TPU v7x, 32 devices: a whole 2x2x4 slice. The times are simulated.
32 devices in a mesh: ctx: 8 (over z, x), head: 4 (over y, core).
Axes of the slice: x: 2, y: 2, z: 4, core: 2. Of those that a mesh axis runs over, the one named last changes fastest.
Arguments:
- lin_query: bfloat16 [2048, 256], P('ctx', 'head'), may hold values from -4 to 4
- lin_key: bfloat16 [2048, 256], P('ctx', 'head'), may hold values from -3 to 3
- lin_values: bfloat16 [2048, 2048], P('ctx', 'head'), may hold values from -43 to 43
- win_query: bfloat16 [2048, 2048], P('ctx', 'head'), may hold values from -30 to 30
- win_key: bfloat16 [2048, 2048], P('ctx', 'head'), may hold values from -30 to 30
- win_value: bfloat16 [2048, 2048], P('ctx', 'head'), may hold values from -4 to 4
- conv_weight: bfloat16 [3, 2048], P(None, 'head'), may hold values from -3 to 3
- head_gain: float32 [2048], P('head'), may hold values from 0.7 to 12.6
Outputs:
- mixed_out: bfloat16 [2048, 2048], P('ctx', 'head')
All inputs are finite; a program needn't handle non-finite values.
Results may differ from a plain program's by a relative error of at most 0.0019.
Values may be sent and summed in bfloat16 or wider, within the bound.
A program may use at most 192 MiB of HBM per device.

v0:
```python
import math

import jax
import jax.numpy as jnp
from jax import lax
from jax.sharding import PartitionSpec as P

FDIM = 16
VDIM = 128
WIN = 64
TAPS = 3
D = 2048


def carried_in(part, axis, combine, identity):
    place = lax.axis_index(axis)
    gathered = jax.tree.map(lambda a: lax.all_gather(a, axis), part)
    state = jax.tree.map(lambda a, e: jnp.zeros_like(a) + jnp.asarray(e, a.dtype), part, identity)

    def one(hop, state):
        return combine(
            state, jax.tree.map(lambda a: lax.dynamic_index_in_dim(a, hop, 0, False), gathered)
        )

    return lax.fori_loop(0, place, one, state)


def passed_along(shard, axis, by):
    length = lax.axis_size(axis)
    pairs = [(i, i + by) for i in range(length) if 0 <= i + by < length]
    return lax.ppermute(shard, axis, pairs)


def features_outer(x_tok):
    xt = jnp.transpose(x_tok.astype(jnp.float32), (1, 2, 0))
    heads, fdim, count = xt.shape
    ones = jnp.ones((heads, 1, count), jnp.float32)
    outer = (xt[:, :, None, :] * xt[:, None, :, :]).reshape(heads, fdim * fdim, count) * (
        1.0 / math.sqrt(32.0)
    )
    return jnp.concatenate([ones, xt * 0.5, outer], axis=1)


def add_states(earlier, later):
    return (earlier[0] + later[0], earlier[1] + later[1])


def window_slab(query, key_ext, value_ext, start):
    count, width = query.shape
    heads = width // VDIM
    blocks = count // WIN
    qb = query.reshape(blocks, WIN, heads, VDIM)
    keys = jnp.concatenate(
        [
            key_ext[:count].reshape(blocks, WIN, heads, VDIM),
            key_ext[WIN:].reshape(blocks, WIN, heads, VDIM),
        ],
        axis=1,
    )
    vals = jnp.concatenate(
        [
            value_ext[:count].reshape(blocks, WIN, heads, VDIM),
            value_ext[WIN:].reshape(blocks, WIN, heads, VDIM),
        ],
        axis=1,
    )
    scores = jnp.einsum("bihe,bjhe->bhij", qb, keys, preferred_element_type=jnp.float32) * (
        1.0 / math.sqrt(VDIM)
    )
    rows_i = jnp.arange(WIN, dtype=jnp.int32)[:, None]
    cols_j = jnp.arange(2 * WIN, dtype=jnp.int32)[None, :]
    block_ids = jnp.arange(blocks, dtype=jnp.int32)[:, None, None]
    position = start + block_ids * WIN + cols_j[None] - WIN
    allowed = (cols_j > rows_i)[None] & (cols_j <= rows_i + WIN)[None] & (position >= 0)
    allowed = allowed[:, None]
    top = jnp.max(jnp.where(allowed, scores, jnp.float32(-1e30)), axis=-1, keepdims=True)
    prob = jnp.where(allowed, jnp.exp(scores - top), jnp.float32(0.0))
    total = jnp.sum(prob, axis=-1)
    out = jnp.einsum(
        "bhij,bjhe->bihe", prob.astype(jnp.bfloat16), vals, preferred_element_type=jnp.float32
    )
    out = out / jnp.transpose(total, (0, 2, 1))[..., None]
    return out.reshape(count, width)


def inner_causal(queries, keys, values):
    count = queries.shape[0]
    block_rows = min(512, count)
    sim = jnp.einsum("thf,shf->hts", queries, keys, preferred_element_type=jnp.float32) * 0.25
    row_pos = 0 + jnp.arange(block_rows, dtype=jnp.int32)
    causal = row_pos[:, None] >= jnp.arange(block_rows, dtype=jnp.int32)[None, :]
    weights = jnp.where(causal[None], 1.0 + sim + 0.5 * sim * sim, jnp.float32(0.0))
    denom_parts = jnp.sum(weights, axis=-1)
    numer_parts = jnp.einsum(
        "hts,shv->htv", weights.astype(jnp.bfloat16), values, preferred_element_type=jnp.float32
    )
    return (numer_parts, denom_parts)


def body(lin_query, lin_key, lin_values, win_query, win_key, win_value, conv_weight, head_gain):
    count = lin_query.shape[0]
    heads = lin_query.shape[1] // FDIM
    queries = lin_query.reshape(count, heads, FDIM)
    keys = lin_key.reshape(count, heads, FDIM)
    values = lin_values.reshape(count, heads, VDIM)
    values32 = values.astype(jnp.float32)
    phi_q = features_outer(queries)
    phi_k = features_outer(keys)
    local_state = jnp.einsum("hft,thv->hfv", phi_k, values32, precision=lax.Precision.HIGHEST)
    local_norm = jnp.sum(phi_k, axis=-1)
    empty = (jnp.zeros_like(local_state), jnp.zeros_like(local_norm))
    prior_state, prior_norm = carried_in((local_state, local_norm), "ctx", add_states, empty)
    start = lax.axis_index("ctx") * count
    rims = passed_along((win_key[count - WIN :], win_value[count - WIN :]), "ctx", 1)
    key_ext = jnp.concatenate([rims[0], win_key], axis=0)
    value_ext = jnp.concatenate([rims[1], win_value], axis=0)
    window_out = window_slab(win_query, key_ext, value_ext, start)
    taps = conv_weight.astype(jnp.float32)
    value_f32 = value_ext.astype(jnp.float32)
    conv_out = jnp.zeros((count, value_ext.shape[1]), jnp.float32)
    for tap in range(TAPS):
        conv_out = conv_out + taps[tap][None, :] * value_f32[WIN - tap : WIN - tap + count]
    inner_num, inner_den = inner_causal(queries, keys, values)
    numer = inner_num + jnp.einsum(
        "hft,hfv->htv", phi_q, prior_state, precision=lax.Precision.HIGHEST
    )
    denom = inner_den + jnp.einsum("hft,hf->ht", phi_q, prior_norm, precision=lax.Precision.HIGHEST)
    lin_out = jnp.transpose(numer / denom[..., None], (1, 0, 2)).reshape(count, heads * VDIM)
    mixed = head_gain[None, :] * (lin_out + window_out + conv_out)
    squares = lax.psum(jnp.sum(mixed * mixed, axis=-1), "head")
    msq = squares / D
    return (mixed * lax.rsqrt(msq + 1e-06)[:, None]).astype(jnp.bfloat16)


def solution(mesh):
    placed = (
        P("ctx", "head"),
        P("ctx", "head"),
        P("ctx", "head"),
        P("ctx", "head"),
        P("ctx", "head"),
        P("ctx", "head"),
        P(None, "head"),
        P("head"),
    )
    return jax.shard_map(
        body, mesh=mesh, in_specs=placed, out_specs=P("ctx", "head"), check_vma=False
    )
```

profile of v0, /device:TPU:26, one launch (start us, length us, event | category | flops | bytes accessed | tf_op | source)
XLA Modules:
  0.0 120.0 jit_solution(16888376617695391166)
XLA Ops:
  6.5 0.8 convert_bitcast_fusion
  7.3 0.8 broadcast_multiply_fusion
  8.1 0.1 multiply_multiply_fusion
  8.3 0.0 copy-start.2
  8.3 0.0 copy-start.1
  8.3 0.0 copy-start.10
  8.3 0.0 copy-start.6
  8.3 0.0 copy-start.7
  8.3 1.6 %fusion.9 = f32[4,273,128]{2,1,0:T(8,128)} fusion(f32[4,256,256]{2,1,0:T(8,128)S(1)} %bitcast.74, f32[4,16,256]{2,1,0:T(8,128)S(1)} %broadcast_multiply_fusion, f32[273]{0:T(512)S(1)} %pad.9.clone, bf16[256,512]{1,0:T(8,128)(2,1)S(1)} %copy-done), kind=kOutput, calls=%fused_computation.19 | convolution fusion | flops 429950976 | bytes 1936452 | tf_op jit(solution)/shard_map/hft,thv->hfv/dot_general | solution.py:109
  10.0 0.0 all-gather.5.cloned.1.call-update
  10.0 0.6 slice.32
  10.6 1.3 %collective-permute-start.1 = (bf16[64,512]{1,0:T(8,128)(2,1)}, bf16[64,512]{1,0:T(8,128)(2,1)}, u32[]{:S(2)}, u32[]{:S(2)}) collective-permute-start(bf16[64,512]{1,0:T(8,128)(2,1)} %slice.32), channel_id=1, source_target_pairs={{0,4},{4,8},{8,12},{12,16},{16,20},{20,24},{24,28},{1,5},{5,9},{9,... | collective-permute-start | bytes 196616 | tf_op jit(solution)/shard_map/ppermute | solution.py:31
  11.9 1.3 %collective-permute-start = (bf16[64,512]{1,0:T(8,128)(2,1)S(1)}, bf16[64,512]{1,0:T(8,128)(2,1)S(1)}, u32[]{:S(2)}, u32[]{:S(2)}) collective-permute-start(bf16[64,512]{1,0:T(8,128)(2,1)S(1)} %slice.30), channel_id=1, source_target_pairs={{0,4},{4,8},{8,12},{12,16},{16,20},{20,24},{24,28},{1,5},{5,9},{9,... | collective-permute-start | bytes 196616 | tf_op jit(solution)/shard_map/ppermute | solution.py:31
  13.3 0.1 add_compare_fusion
  13.4 0.1 fusion.39
  13.5 0.6 fusion.53
  14.1 0.6 broadcast_and_fusion
  14.7 0.6 broadcast_multiply_fusion.1
  15.3 1.1 fusion.54
  16.5 0.1 multiply_multiply_fusion.1
  16.6 1.1 fusion.25
  17.7 0.5 fusion.8
  18.2 0.1 reshape.142
  18.2 0.1 reshape.140
  18.4 0.3 copy-done.4
  18.7 0.8 reshape.143
  19.5 34.2 %all-gather.2 = f32[8,4,273]{2,1,0:T(4,128)} all-gather(f32[1,4,273]{2,1,0:T(4,128)S(1)} %bitcast.84), channel_id=3, replica_groups=mesh['ctx'=8,'head'=4] {'ctx'}, dimensions={0}, use_global_device_ids=true | all-gather | bytes 39312 | tf_op jit(solution)/shard_map/all_gather | solution.py:17
  53.7 0.0 collective-permute-done
  53.8 0.1 convert_element_type.21
  53.8 0.0 collective-permute-done.1
  53.8 0.9 pad_maximum_fusion.5
  54.7 0.0 copy-start.5
  54.7 0.1 reshape.141
  54.8 0.1 reshape.139
  55.0 0.7 copy-done.5
  55.7 0.5 fusion.7
  56.1 0.0 copy-done.9
  56.1 0.4 fusion.55
  56.5 0.4 copy-done.15
  56.9 1.6 %fusion.6 = f32[4,64,4,128]{3,1,2,0:T(8,128)S(1)} fusion(bf16[4,64,4,128]{3,1,2,0:T(8,128)(2,1)S(1)} %copy.28, bf16[4,64,4,128]{3,1,2,0:T(8,128)(2,1)S(1)} %copy.27, f32[4,64,4]{1,2,0:T(4,128)S(1)} %bitcast.88, f32[4,4,64,128]{3,2,1,0:T(8,128)} %copy-done.15, pred[4,64,128]{2,1,0:T(8,128)(4,1)} %broadcast_and_fusion), kind=kOutput, calls=%fused_computation.10 | convolution fusion | flops 35259520 | bytes 1609728 | tf_op jit(solution)/shard_map/bhij,bjhe->bihe/dot_general | solution.py:79
  58.6 0.3 copy.32
  58.9 28.2 %all-gather.5.cloned.1.call-done = f32[32,273,128]{2,1,0:T(8,128)} async-done(((f32[4,273,128]{2,1,0:T(8,128)}), f32[32,273,128]{2,1,0:T(8,128)}) %all-gather.5.cloned.1.call-update) | async-done | bytes 4472848 | tf_op jit(solution)/shard_map/all_gather | solution.py:17
  87.1 13.2 %while.12 = (s32[]{:T(128)}, f32[4,273,128]{2,1,0:T(8,128)S(1)}, f32[4,273]{1,0:T(4,128)S(1)}, s32[]{:T(128)}, f32[8,4,273,128]{3,2,1,0:T(8,128)}, /*index=5*/f3...) while((s32[]{:T(128)}, f32[4,273,128]{2,1,0:T(8,128)S(1)}, f32[4,273]{1,0:T(4,128)S(1)}, s32[]{:T(128)}, ...), condition=%wide.region_2.3_spmd, body=%wide.region_1.2_spmd.sunk | while | flops 140873 | bytes 1690551 | solution.py:25
  87.1 1.2 bitcast_add_fusion.6
  88.3 0.7 bitcast_add_fusion.7
  89.0 1.2 bitcast_add_fusion.6
  90.2 0.7 bitcast_add_fusion.7
  90.9 1.2 bitcast_add_fusion.6
  92.1 0.7 bitcast_add_fusion.7
  92.8 1.2 bitcast_add_fusion.6
  94.0 0.7 bitcast_add_fusion.7
  94.7 1.2 bitcast_add_fusion.6
  95.9 0.7 bitcast_add_fusion.7
  96.6 1.2 bitcast_add_fusion.6
  97.7 0.7 bitcast_add_fusion.7
  98.5 1.2 bitcast_add_fusion.6
  99.6 0.7 bitcast_add_fusion.7
  100.4 0.9 fusion.10
  101.3 0.1 copy-done.3
  101.4 2.5 %fusion.2 = f32[256,4,128]{0,2,1:T(8,128)} fusion(f32[4,256,128]{1,2,0:T(8,128)S(1)} %copy-done.3, f32[4,273,128]{2,1,0:T(8,128)S(1)} %get-tuple-element.39, f32[4,256,256]{2,1,0:T(8,128)S(1)} %bitcast.79, f32[4,16,256]{2,1,0:T(8,128)S(1)} %copy-done.8, f32[273]{0:T(512)S(1)} %pad.9.clone, f32[256,4]{0,1:T(4,128)S(1)} %fusion.41), kind=kOutput, calls=%fused_computation.6 | convolution fusion | flops 430213120 | bytes 2726980 | tf_op jit(solution)/shard_map/hft,hfv->htv/dot_general | solution.py:124
  103.9 1.2 %copy.33 = f32[256,512]{1,0:T(8,128)S(1)} copy(f32[256,512]{0,1:T(8,128)} %bitcast.80) | data formatting | bytes 1048576 | tf_op jit(solution)/shard_map/reshape | solution.py:128
  105.2 0.3 multiply_reduce_fusion
  105.5 6.9 %psum.7 = f32[256]{0:T(256)S(1)} all-reduce(f32[256]{0:T(256)S(1)} %get-tuple-element.53), channel_id=1, replica_groups=mesh['ctx'=8,'head'=4] {'head'}, use_global_device_ids=true, to_apply=%region_7.8 | all-reduce | flops 256 | bytes 2048 | tf_op jit(solution)/shard_map/psum | solution.py:130
  112.4 0.8 multiply_convert_fusion
  (39 shorter events, 0.4 us)
Async XLA Ops:
  6.5 1.7 %copy-start = (bf16[256,512]{1,0:T(8,128)(2,1)S(1)}, bf16[256,512]{1,0:T(8,128)(2,1)}, u32[]{:S(2)}) copy-start(bf16[256,512]{1,0:T(8,128)(2,1)} %param.12) | copy-start | bytes 786436
  6.5 80.5 %all-gather.5.cloned.1.call-start = ((), (), s32[]{:S(2)}) async-start(), calls=%async_computation | async-start | bytes 5160960 | tf_op jit(solution)/shard_map/all_gather | solution.py:17
  8.3 1.7 %copy-start.2 = (bf16[256,512]{1,0:T(8,128)(2,1)S(1)}, bf16[256,512]{1,0:T(8,128)(2,1)}, u32[]{:S(2)}) copy-start(bf16[256,512]{1,0:T(8,128)(2,1)} %param.14) | copy-start | bytes 786436
  8.3 3.6 %copy-start.1 = (bf16[256,512]{1,0:T(8,128)(2,1)S(1)}, bf16[256,512]{1,0:T(8,128)(2,1)}, u32[]{:S(2)}) copy-start(bf16[256,512]{1,0:T(8,128)(2,1)} %param.15) | copy-start | bytes 786436
  8.3 5.2 %copy-start.10 = (bf16[3,512]{1,0:T(4,128)(2,1)S(1)}, bf16[3,512]{1,0:T(4,128)(2,1)}, u32[]{:S(2)}) copy-start(bf16[3,512]{1,0:T(4,128)(2,1)} %param.16) | copy-start | bytes 9220
  8.3 6.4 %copy-start.6 = (bf16[256,64]{0,1:T(8,128)(2,1)S(1)}, bf16[256,64]{0,1:T(8,128)(2,1)}, u32[]{:S(2)}) copy-start(bf16[256,64]{0,1:T(8,128)(2,1)} %param.10) | copy-start | bytes 98308
  8.3 7.0 %copy-start.7 = (bf16[256,64]{0,1:T(8,128)(2,1)S(1)}, bf16[256,64]{0,1:T(8,128)(2,1)}, u32[]{:S(2)}) copy-start(bf16[256,64]{0,1:T(8,128)(2,1)} %param.11) | copy-start | bytes 98308
  10.6 43.2 %collective-permute-start.1 = (bf16[64,512]{1,0:T(8,128)(2,1)}, bf16[64,512]{1,0:T(8,128)(2,1)}, u32[]{:S(2)}, u32[]{:S(2)}) collective-permute-start(bf16[64,512]{1,0:T(8,128)(2,1)} %slice.32), channel_id=1, source_target_pairs={{0,4},{4,8},{8,12},{12,16},{16,20},{20,24},{24,28},{1,5},{5,9},{9,... | collective-permute-start | bytes 196616 | tf_op jit(solution)/shard_map/ppermute | solution.py:31
  11.9 41.8 %collective-permute-start = (bf16[64,512]{1,0:T(8,128)(2,1)S(1)}, bf16[64,512]{1,0:T(8,128)(2,1)S(1)}, u32[]{:S(2)}, u32[]{:S(2)}) collective-permute-start(bf16[64,512]{1,0:T(8,128)(2,1)S(1)} %slice.30), channel_id=1, source_target_pairs={{0,4},{4,8},{8,12},{12,16},{16,20},{20,24},{24,28},{1,5},{5,9},{9,... | collective-permute-start | bytes 196616 | tf_op jit(solution)/shard_map/ppermute | solution.py:31
  17.7 1.0 copy-start.4
  54.7 1.0 copy-start.5
  54.9 1.2 %copy-start.9 = (pred[4,64,128]{2,1,0:T(8,128)(4,1)S(1)}, pred[4,64,128]{2,1,0:T(8,128)(4,1)}, u32[]{:S(2)}) copy-start(pred[4,64,128]{2,1,0:T(8,128)(4,1)} %broadcast_and_fusion) | copy-start | bytes 98308
  56.1 0.8 copy-start.15
  87.1 13.2 %copy-start.8 = (f32[4,16,256]{2,1,0:T(8,128)S(1)}, f32[4,16,256]{2,1,0:T(8,128)}, u32[]{:S(2)}) copy-start(f32[4,16,256]{2,1,0:T(8,128)} %broadcast_multiply_fusion.1) | copy-start | bytes 196612
  100.3 1.0 copy-start.13
  100.3 1.0 copy-start.3
  101.4 3.7 %copy-start.11 = (f32[1,512]{1,0:T(1,128)S(1)}, f32[1,512]{1,0:T(1,128)}, u32[]{:S(2)}) copy-start(f32[1,512]{1,0:T(1,128)} %get-tuple-element.56) | copy-start | bytes 6148
  101.4 3.7 %copy-start.12 = (f32[1,512]{1,0:T(1,128)S(1)}, f32[1,512]{1,0:T(1,128)}, u32[]{:S(2)}) copy-start(f32[1,512]{1,0:T(1,128)} %get-tuple-element.57) | copy-start | bytes 6148
  101.4 3.8 %copy-start.14 = (f32[512]{0:T(512)S(1)}, f32[512]{0:T(512)}, u32[]{:S(2)}) copy-start(f32[512]{0:T(512)} %param.17) | copy-start | bytes 6148
Sparse Core Ops, SparseCore 0:
  10.1 76.8 all-gather.4
where the time goes:
time: 121 us; the launch traced here: 120 us
  blocking collectives  41.1 us (34%)
  waiting for transfers between devices  28.2 us (23%)
  other arithmetic  19.4 us (16%)
  between operations  13.8 us (11%)
  matrix products  9.32 us (8%)
  local copies, waits for them, and re-layouts  5.66 us (5%)
  starting transfers between devices  2.57 us (2%)
    all_gather x1, blocking collectives, carried_in(): gathered = jax.tree.map(lambda a: lax.all_gather(a, axis), part)  34.2 us
    all_gather x1, waiting for transfers between devices, carried_in(): gathered = jax.tree.map(lambda a: lax.all_gather(a, axis), part)  28.2 us
    add x14, other arithmetic, add_states(): return (earlier[0] + later[0], earlier[1] + later[1])  13.2 us
    psum x1, blocking collectives, body(): squares = lax.psum(jnp.sum(mixed * mixed, axis=-1), 'head')  6.86 us
    ppermute x2, starting transfers between devices, passed_along(): return lax.ppermute(shard, axis, pairs)  2.57 us
    dot_general x1, matrix products, body(): jnp.einsum('hft,hfv->htv', phi_q, prior_state, precision=lax.Precision.HI...  2.49 us
  transfers between devices with their start and end apart: 3, of which 1 were waited for; matrix products, arithmetic and copies ran while one was open for 9% of the time, Pallas kernels for 0%

commit v1 on v0

v1 whole, which is shorter than its diff:
```python
import functools

import jax
import jax.numpy as jnp
import numpy as np
from jax import lax
from jax.experimental import pallas as pl
from jax.experimental.pallas import tpu as pltpu
from jax.sharding import PartitionSpec as P

FDIM = 16
VDIM = 128
WIN = 64
TAPS = 3
BLK = 128
PAIRS = [(i, j) for i in range(FDIM) for j in range(i, FDIM)]
NP = len(PAIRS)
ONE = NP + FDIM
ROWS = ONE + 8
MESH = pl.DeviceIdType.MESH
F32 = jnp.float32
BF16 = jnp.bfloat16
NT = (((1,), (1,)), ((), ()))


def selectors(heads):
    first = np.zeros((FDIM, 256), np.float32)
    second_q = np.zeros((FDIM, 256), np.float32)
    second_k = np.zeros((FDIM, NP), np.float32)
    for f, (i, j) in enumerate(PAIRS):
        first[i, f] = 1.0
        second_k[j, f] = 1.0
        second_q[j, f] = 1.0 / 32.0 if i == j else 1.0 / 16.0
    for i in range(FDIM):
        first[i, NP + i] = 1.0
    rep = lambda a: np.tile(a, (heads, 1))
    return (
        jnp.asarray(rep(first), BF16),
        jnp.asarray(rep(second_q), BF16),
        jnp.asarray(rep(first[:, :ONE]).T, BF16),
        jnp.asarray(rep(second_k).T, BF16),
    )


def encode(x):
    tile = x[ONE:]
    keep = lax.broadcasted_iota(jnp.int32, tile.shape, 0) < 3
    hi = tile.astype(BF16).astype(F32)
    low = jnp.where(keep, tile - hi, 0.0)
    tile = jnp.where(keep, hi, 0.0) + pltpu.roll(low, 3, 0)
    return jnp.concatenate([x[:ONE], tile], axis=0).astype(BF16)


def decode(x):
    x = x.astype(F32)
    tile = x[ONE:]
    keep = lax.broadcasted_iota(jnp.int32, tile.shape, 0) < 3
    tile = jnp.where(keep, tile + pltpu.roll(tile, 5, 0), 0.0)
    return jnp.concatenate([x[:ONE], tile], axis=0)


def kernel(
    n, nh, heads, total_width,
    lq_ref, lk_ref, lv_ref, wq_ref, wk_ref, wv_ref, cw_ref, hg_ref, e1q_ref, e2q_ref, e1k_ref, e2k_ref,
    out_ref,
    own, zin, xin, fwd, hk, hv, mix, num, den, sq_out, sq_in,
    z_send, z_recv, x_send, x_recv, h_send, h_recv, s_send, s_recv,
):
    count = lq_ref.shape[0]
    ctx = lax.axis_index("ctx")
    hd = lax.axis_index("head")
    z = ctx // 2
    x = lax.rem(ctx, 2)
    nz = n // 2
    partner = ctx + 1 - 2 * x

    barrier = pltpu.get_barrier_semaphore()

    peers = jnp.minimum(ctx, 2) + jnp.minimum(n - 1 - ctx, 2) + (nh - 1)

    def greet(c, h):
        pl.semaphore_signal(barrier, inc=1, device_id=(c, h), device_id_type=MESH)

    for by in (-2, -1, 1, 2):
        @pl.when((ctx + by >= 0) & (ctx + by < n))
        def _(by=by):
            greet(ctx + by, hd)
    for j in range(1, nh):
        greet(ctx, lax.rem(hd + j, nh))

    lane_head = lax.broadcasted_iota(jnp.int32, (count, heads * FDIM), 1) // FDIM
    lk = lk_ref[...]
    lq = lq_ref[...]
    zero = jnp.zeros((), BF16)

    row8 = lax.broadcasted_iota(jnp.int32, (8, VDIM), 0)
    ones = jnp.ones((8, count), BF16)
    const = jnp.where(lax.broadcasted_iota(jnp.int32, (8, count), 0) == 0, 1.0, 0.0)
    for h in range(heads):
        kh = jnp.where(lane_head == h, lk, zero)
        a = lax.dot_general(e1k_ref[...], kh, NT, preferred_element_type=F32)
        b = lax.dot_general(e2k_ref[...], kh, NT, preferred_element_type=F32)
        phi = jnp.concatenate([a[:NP] * b, a[NP:], const], axis=0).astype(BF16)
        st = jnp.dot(phi, lv_ref[:, h * VDIM:(h + 1) * VDIM], preferred_element_type=F32)
        n_a = lax.dot_general(ones, phi[:VDIM], NT, preferred_element_type=F32)
        rest = jnp.concatenate([phi[VDIM:], jnp.zeros((2 * VDIM - ROWS, count), BF16)], axis=0)
        n_b = lax.dot_general(ones, rest, NT, preferred_element_type=F32)
        tile = st[ONE:] + jnp.where(row8 == 1, n_a, 0.0) + jnp.where(row8 == 2, n_b, 0.0)
        own[h] = jnp.concatenate([st[:ONE], tile], axis=0)

    pl.semaphore_wait(barrier, peers)

    def halo(src, dst, i):
        return pltpu.make_async_remote_copy(
            src_ref=src.at[pl.ds(count - WIN, WIN)], dst_ref=dst,
            send_sem=h_send.at[i], recv_sem=h_recv.at[i],
            device_id=(ctx + 1, hd), device_id_type=MESH)

    def z_copy(h):
        return pltpu.make_async_remote_copy(
            src_ref=fwd.at[h], dst_ref=zin.at[h], send_sem=z_send.at[h], recv_sem=z_recv.at[h],
            device_id=(ctx + 2, hd), device_id_type=MESH)

    def x_copy(h, src):
        return pltpu.make_async_remote_copy(
            src_ref=src.at[h], dst_ref=xin.at[h], send_sem=x_send.at[h], recv_sem=x_recv.at[h],
            device_id=(partner, hd), device_id_type=MESH)

    @pl.when(ctx < n - 1)
    def _():
        halo(wk_ref, hk, 0).start()
        halo(wv_ref, hv, 1).start()

    @pl.when(ctx == 0)
    def _():
        hk[...] = jnp.zeros_like(hk)
        hv[...] = jnp.zeros_like(hv)

    def send(h):
        @pl.when(z < nz - 1)
        def _():
            z_copy(h).start()

        @pl.when(x == 0)
        def _():
            x_copy(h, fwd).start()

    def first_chain():
        for h in range(heads):
            fwd[h] = encode(own[h])
            send(h)

    def chain():
        for h in range(heads):
            z_copy(h).wait_recv()

            @pl.when(x == 1)
            def _(h=h):
                x_copy(h, zin).start()

            fwd[h] = encode(decode(zin[h]) + own[h])
            send(h)

    pl.when(z == 0)(first_chain)
    pl.when(z == 1)(chain)

    row_i = lax.broadcasted_iota(jnp.int32, (count, count), 0)
    col_i = lax.broadcasted_iota(jnp.int32, (count, count), 1)
    causal = row_i >= col_i
    wr = lax.broadcasted_iota(jnp.int32, (BLK, BLK + WIN), 0)
    wc = lax.broadcasted_iota(jnp.int32, (BLK, BLK + WIN), 1)
    band = (wc > wr) & (wc <= wr + WIN)

    def inner(h):
        cols = slice(h * VDIM, (h + 1) * VDIM)
        kh = jnp.where(lane_head == h, lk, zero)
        s = lax.dot_general(lq, kh, NT, preferred_element_type=F32) * 0.25
        a = jnp.where(causal, 1.0 + s + 0.5 * s * s, 0.0)
        den[h] = jnp.sum(a, axis=-1, keepdims=True)
        num[:, cols] = jnp.dot(a.astype(BF16), lv_ref[:, cols], preferred_element_type=F32)

    def window(h, b, ext_k, ext_v, allowed):
        cols = slice(h * VDIM, (h + 1) * VDIM)
        rows = slice(b * BLK, (b + 1) * BLK)
        s = lax.dot_general(wq_ref[rows, cols], ext_k, NT, preferred_element_type=F32) * (1.0 / np.sqrt(VDIM))
        top = jnp.max(jnp.where(allowed, s, -1e30), axis=-1, keepdims=True)
        p = jnp.where(allowed, jnp.exp(s - top), 0.0)
        tot = jnp.sum(p, axis=-1, keepdims=True)
        o = jnp.dot(p.astype(BF16), ext_v, preferred_element_type=F32)
        mix[rows, cols] = o / tot

    def later_blocks(h):
        cols = slice(h * VDIM, (h + 1) * VDIM)
        for b in range(1, count // BLK):
            rows = slice(b * BLK - WIN, (b + 1) * BLK)
            window(h, b, wk_ref[rows, cols], wv_ref[rows, cols], band)

    def first_block(h):
        cols = slice(h * VDIM, (h + 1) * VDIM)
        ext_k = jnp.concatenate([hk[:, cols], wk_ref[:BLK, cols]], axis=0)
        ext_v = jnp.concatenate([hv[:, cols], wv_ref[:BLK, cols]], axis=0)
        window(h, 0, ext_k, ext_v, band & ((wc >= WIN) | (ctx > 0)))

    def conv(h):
        cols = slice(h * VDIM, (h + 1) * VDIM)
        ext = jnp.concatenate([hv[WIN - 16:, cols], wv_ref[:, cols]], axis=0).astype(F32)
        taps = cw_ref[:, cols].astype(F32)
        acc = taps[0:1] * ext[16:16 + count]
        for t in range(1, TAPS):
            acc = acc + taps[t:t + 1] * ext[16 - t:16 - t + count]
        mix[:, cols] += acc

    for h in range(heads):
        inner(h)
    pl.when(z == 2)(chain)
    for h in range(heads):
        later_blocks(h)

    @pl.when(ctx > 0)
    def _():
        halo(wk_ref, hk, 0).wait_recv()
        halo(wv_ref, hv, 1).wait_recv()

    for h in range(heads):
        first_block(h)
        conv(h)
    if nz > 3:
        pl.when(z > 2)(chain)

    lane = lax.broadcasted_iota(jnp.int32, (1, 256), 1)
    add1 = jnp.where(lane == ONE, 1.0, 0.0)
    add2 = jnp.where(lane == ONE, 1.0, jnp.where((lane >= NP) & (lane < ONE), 0.25, 0.0))
    squares = jnp.zeros((count, VDIM), F32)
    for h in range(heads):
        cols = slice(h * VDIM, (h + 1) * VDIM)
        qh = jnp.where(lane_head == h, lq, zero)
        a = jnp.dot(qh, e1q_ref[...], preferred_element_type=F32) + add1
        b = jnp.dot(qh, e2q_ref[...], preferred_element_type=F32) + add2
        phi = a * b

        @pl.when(ctx > 0)
        def _():
            x_copy(h, zin).wait_recv()

            @pl.when(z > 0)
            def _():
                own[h] = decode(zin[h]) + decode(xin[h])

            @pl.when(z == 0)
            def _():
                own[h] = decode(xin[h])

        @pl.when(ctx == 0)
        def _():
            own[h] = jnp.zeros((ROWS, VDIM), F32)

        st = own[h]
        tile = st[ONE:]
        norm = jnp.concatenate([tile[1:2], tile[2:3]], axis=1)
        state = jnp.concatenate([st[:ONE], jnp.zeros((8, VDIM), F32)], axis=0)
        phi_n = phi[:, :ROWS]
        p_hi = phi_n.astype(BF16)
        p_lo = (phi_n - p_hi.astype(F32)).astype(BF16)
        s_hi = state.astype(BF16)
        s_lo = (state - s_hi.astype(F32)).astype(BF16)
        cross = (
            jnp.dot(p_hi, s_hi, preferred_element_type=F32)
            + jnp.dot(p_hi, s_lo, preferred_element_type=F32)
            + jnp.dot(p_lo, s_hi, preferred_element_type=F32)
        )
        d = den[h] + jnp.sum(phi * norm, axis=-1, keepdims=True)
        lin = (num[:, cols] + cross + tile[0:1]) / d
        m = hg_ref[:, cols] * (lin + mix[:, cols])
        mix[:, cols] = m
        squares = squares + m * m

    row = jnp.sum(squares.T, axis=0, keepdims=True)
    sq_out[...] = jnp.broadcast_to(row, sq_out.shape)

    def sq_copy(j):
        return pltpu.make_async_remote_copy(
            src_ref=sq_out, dst_ref=sq_in.at[j - 1], send_sem=s_send.at[j - 1], recv_sem=s_recv.at[j - 1],
            device_id=(ctx, lax.rem(hd + j, nh)), device_id_type=MESH)

    for j in range(1, nh):
        sq_copy(j).start()
    tot = sq_out[...]
    for j in range(1, nh):
        sq_copy(j).wait_recv()
        tot = tot + sq_in[j - 1]
    scale = lax.rsqrt(tot * (1.0 / total_width) + 1e-6)
    scale = jnp.broadcast_to(scale[0:1], (VDIM, count)).T
    for h in range(heads):
        cols = slice(h * VDIM, (h + 1) * VDIM)
        out_ref[:, cols] = (mix[:, cols] * scale).astype(BF16)

    for j in range(1, nh):
        sq_copy(j).wait_send()

    @pl.when(ctx < n - 1)
    def _():
        halo(wk_ref, hk, 0).wait_send()
        halo(wv_ref, hv, 1).wait_send()

    for h in range(heads):
        @pl.when(z < nz - 1)
        def _(h=h):
            z_copy(h).wait_send()

        @pl.when((x == 0) | (z > 0))
        def _(h=h):
            x_copy(h, zin).wait_send()


def body(n, nh, lq, lk, lv, wq, wk, wv, cw, hg):
    count, width = wv.shape
    heads = width // VDIM
    vmem = pl.BlockSpec(memory_space=pltpu.VMEM)
    dma = pltpu.SemaphoreType.DMA
    call = pl.pallas_call(
        functools.partial(kernel, n, nh, heads, width * nh),
        out_shape=jax.ShapeDtypeStruct((count, width), BF16),
        in_specs=[vmem] * 12,
        out_specs=vmem,
        scratch_shapes=[
            pltpu.VMEM((heads, ROWS, VDIM), F32),
            pltpu.VMEM((heads, ROWS, VDIM), BF16),
            pltpu.VMEM((heads, ROWS, VDIM), BF16),
            pltpu.VMEM((heads, ROWS, VDIM), BF16),
            pltpu.VMEM((WIN, width), BF16),
            pltpu.VMEM((WIN, width), BF16),
            pltpu.VMEM((count, width), F32),
            pltpu.VMEM((count, width), F32),
            pltpu.VMEM((heads, count, 1), F32),
            pltpu.VMEM((8, count), F32),
            pltpu.VMEM((nh - 1, 8, count), F32),
            dma((heads,)), dma((heads,)), dma((heads,)), dma((heads,)),
            dma((2,)), dma((2,)), dma((nh - 1,)), dma((nh - 1,)),
        ],
        compiler_params=pltpu.CompilerParams(
            collective_id=0, has_side_effects=True, vmem_limit_bytes=40 * 1024 * 1024
        ),
        cost_estimate=pl.CostEstimate(flops=500_000_000, bytes_accessed=3_000_000, transcendentals=200_000),
    )
    return call(lq, lk, lv, wq, wk, wv, cw, hg.reshape(1, width), *selectors(heads))


def solution(mesh):
    both = P("ctx", "head")
    placed = (both, both, both, both, both, both, P(None, "head"), P("head"))
    return jax.shard_map(
        functools.partial(body, mesh.shape["ctx"], mesh.shape["head"]),
        mesh=mesh, in_specs=placed, out_specs=both, check_vma=False,
    )
```

time: 121 us -> 27.9 us (0.23)
  the two profiles are of different devices: /device:TPU:26 before, /device:TPU:25 now
where the time goes in v1:
time: 27.9 us; the launch traced here: 27.6 us
  Pallas kernels  21.3 us (76%)
  local copies, waits for them, and re-layouts  6.16 us (22%)
    pallas_call x1, Pallas kernels, body(): call(lq, lk, lv, wq, wk, wv, cw, hg.reshape(1, width), *selectors(heads))  21.3 us
    unnamed x25, local copies, waits for them, and re-layouts  6.16 us

profile of v1, /device:TPU:25, one launch (start us, length us, event | category | flops | bytes accessed | tf_op | source)
XLA Modules:
  0.0 27.6 jit_solution(2723181966324782969)
XLA Ops:
  0.0 0.0 copy-start.10
  0.0 0.0 copy-start.8
  0.0 0.0 copy-start.9
  0.0 0.9 %copy.13.lq_ref = bf16[256,64]{1,0:T(8,128)(2,1)S(1)} copy(bf16[256,64]{0,1:T(8,128)(2,1)} %param.12) | data formatting | bytes 65536 | tf_op args[0]
  0.9 0.0 copy-done.10
  0.9 0.0 copy-start.4
  0.9 0.0 copy-start.5
  0.9 0.0 copy-start.6
  0.9 0.0 copy-start.7
  1.0 0.1 copy.14.lk_ref
  1.1 0.0 copy-done.8
  1.1 0.0 copy-done.9
  1.1 0.5 %copy-done.4 = bf16[3,512]{1,0:T(4,128)(2,1)S(1)} copy-done((bf16[3,512]{1,0:T(4,128)(2,1)S(1)}, bf16[3,512]{1,0:T(4,128)(2,1)}, u32[]{:S(2)}) %copy-start.4) | copy-done | bytes 3096
  1.6 0.0 copy-done.5
  1.6 0.1 copy-done.6
  1.7 0.0 copy-done.7
  1.7 0.0 copy-start
  1.7 0.9 %copy-done = bf16[256,512]{1,0:T(8,128)(2,1)S(1)} copy-done((bf16[256,512]{1,0:T(8,128)(2,1)S(1)}, bf16[256,512]{1,0:T(8,128)(2,1)}, u32[]{:S(2)}) %copy-start) | copy-done | bytes 262168
  2.7 0.0 copy-start.1
  2.7 0.9 %copy-done.1 = bf16[256,512]{1,0:T(8,128)(2,1)S(1)} copy-done((bf16[256,512]{1,0:T(8,128)(2,1)S(1)}, bf16[256,512]{1,0:T(8,128)(2,1)}, u32[]{:S(2)}) %copy-start.1) | copy-done | bytes 262168
  3.6 0.0 copy-start.2
  3.6 0.9 %copy-done.2 = bf16[256,512]{1,0:T(8,128)(2,1)S(1)} copy-done((bf16[256,512]{1,0:T(8,128)(2,1)S(1)}, bf16[256,512]{1,0:T(8,128)(2,1)}, u32[]{:S(2)}) %copy-start.2) | copy-done | bytes 262168
  4.6 0.0 copy-start.3
  4.6 0.9 %copy-done.3 = bf16[256,512]{1,0:T(8,128)(2,1)S(1)} copy-done((bf16[256,512]{1,0:T(8,128)(2,1)S(1)}, bf16[256,512]{1,0:T(8,128)(2,1)}, u32[]{:S(2)}) %copy-start.3) | copy-done | bytes 262168
  5.5 21.3 %shard_map.118 = bf16[256,512]{1,0:T(8,128)(2,1)S(1)} custom-call(bf16[256,64]{1,0:T(8,128)(2,1)S(1)} %copy.13.lq_ref, bf16[256,64]{1,0:T(8,128)(2,1)S(1)} %copy.14.lk_ref, bf16[256,512]{1,0:T(8,128)(2,1)S(1)} %copy-done, bf16[256,512]{1,0:T(8,128)(2,1)S(1)} %copy-done.1, bf16[256,512]{1,0:T(8,128)(2,1)S(1)} %copy-done.2, bf16[256,512]{1,0:T(8,128)(2,1)S(1)} %copy-done.3, ...), custom_call_target="tpu_custom_call" | custom-call | flops 500000000 | bytes 3000000 | tf_op jit(solution)/shard_map/pallas_call | solution.py:345
  26.9 0.7 %copy.16 = bf16[256,512]{1,0:T(8,128)(2,1)} copy(bf16[256,512]{1,0:T(8,128)(2,1)S(1)} %shard_map.118) | data formatting | bytes 524288
Async XLA Ops:
  0.0 0.9 %copy-start.10 = (bf16[256,64]{0,1:T(8,128)(2,1)S(1)}, bf16[256,64]{0,1:T(8,128)(2,1)}, u32[]{:S(2)}) copy-start(bf16[256,64]{0,1:T(8,128)(2,1)} %param.13) | copy-start | bytes 98308
  0.0 1.1 %copy-start.8 = (bf16[64,256]{1,0:T(8,128)(2,1)S(1)}, bf16[64,256]{1,0:T(8,128)(2,1)}, u32[]{:S(2)}) copy-start(bf16[64,256]{1,0:T(8,128)(2,1)} %constant.9.clone.e2q_ref) | copy-start | bytes 98308
  0.0 1.1 %copy-start.9 = (bf16[64,256]{1,0:T(8,128)(2,1)S(1)}, bf16[64,256]{1,0:T(8,128)(2,1)}, u32[]{:S(2)}) copy-start(bf16[64,256]{1,0:T(8,128)(2,1)} %constant.8.clone.e1q_ref) | copy-start | bytes 98308
  0.9 0.7 %copy-start.4 = (bf16[3,512]{1,0:T(4,128)(2,1)S(1)}, bf16[3,512]{1,0:T(4,128)(2,1)}, u32[]{:S(2)}) copy-start(bf16[3,512]{1,0:T(4,128)(2,1)} %cw_ref.1) | copy-start | bytes 9220
  0.9 0.7 %copy-start.5 = (f32[512]{0:T(512)S(1)}, f32[512]{0:T(512)}, u32[]{:S(2)}) copy-start(f32[512]{0:T(512)} %param.19) | copy-start | bytes 6148
  0.9 0.8 %copy-start.6 = (bf16[152,64]{1,0:T(8,128)(2,1)S(1)}, bf16[152,64]{1,0:T(8,128)(2,1)}, u32[]{:S(2)}) copy-start(bf16[152,64]{1,0:T(8,128)(2,1)} %constant.10.clone.e1k_ref) | copy-start | bytes 58372
  0.9 0.8 %copy-start.7 = (bf16[136,64]{1,0:T(8,128)(2,1)S(1)}, bf16[136,64]{1,0:T(8,128)(2,1)}, u32[]{:S(2)}) copy-start(bf16[136,64]{1,0:T(8,128)(2,1)} %constant.11.clone.e2k_ref) | copy-start | bytes 52228
  1.7 0.9 %copy-start = (bf16[256,512]{1,0:T(8,128)(2,1)S(1)}, bf16[256,512]{1,0:T(8,128)(2,1)}, u32[]{:S(2)}) copy-start(bf16[256,512]{1,0:T(8,128)(2,1)} %lv_ref.1) | copy-start | bytes 786436
  2.7 0.9 %copy-start.1 = (bf16[256,512]{1,0:T(8,128)(2,1)S(1)}, bf16[256,512]{1,0:T(8,128)(2,1)}, u32[]{:S(2)}) copy-start(bf16[256,512]{1,0:T(8,128)(2,1)} %wq_ref.1) | copy-start | bytes 786436
  3.6 0.9 %copy-start.2 = (bf16[256,512]{1,0:T(8,128)(2,1)S(1)}, bf16[256,512]{1,0:T(8,128)(2,1)}, u32[]{:S(2)}) copy-start(bf16[256,512]{1,0:T(8,128)(2,1)} %wk_ref.1) | copy-start | bytes 786436
  4.6 0.9 %copy-start.3 = (bf16[256,512]{1,0:T(8,128)(2,1)S(1)}, bf16[256,512]{1,0:T(8,128)(2,1)}, u32[]{:S(2)}) copy-start(bf16[256,512]{1,0:T(8,128)(2,1)} %wv_ref.1) | copy-start | bytes 786436

commit v2 on v1

v2 whole, which is shorter than its diff:
```python
import functools

import jax
import jax.numpy as jnp
import numpy as np
from jax import lax
from jax.experimental import pallas as pl
from jax.experimental.pallas import tpu as pltpu
from jax.sharding import PartitionSpec as P

FDIM = 16
VDIM = 128
WIN = 64
TAPS = 3
BLK = 128
PAIRS = [(i, j) for i in range(FDIM) for j in range(i, FDIM)]
NP = len(PAIRS)
ONE = NP + FDIM
ROWS = ONE + 8
EK = ROWS + 144
MESH = pl.DeviceIdType.MESH
F32 = jnp.float32
BF16 = jnp.bfloat16
NT = (((1,), (1,)), ((), ()))


def selectors(heads):
    first = np.zeros((FDIM, 256), np.float32)
    second_q = np.zeros((FDIM, 256), np.float32)
    second_k = np.zeros((FDIM, NP), np.float32)
    for f, (i, j) in enumerate(PAIRS):
        first[i, f] = 1.0
        second_k[j, f] = 1.0
        second_q[j, f] = 1.0 / 32.0 if i == j else 1.0 / 16.0
    for i in range(FDIM):
        first[i, NP + i] = 1.0
    rep = lambda a: np.tile(a, (heads, 1))
    keys = np.zeros((EK, heads * FDIM), np.float32)
    keys[:ONE] = rep(first[:, :ONE]).T
    keys[ROWS:ROWS + NP] = rep(second_k).T
    return (
        jnp.asarray(np.concatenate([rep(f[:, c:c + VDIM]) for f in (first, second_q) for c in (0, VDIM)]), BF16),
        jnp.asarray(keys, BF16),
    )


def encode(x):
    tile = x[ONE:]
    keep = lax.broadcasted_iota(jnp.int32, tile.shape, 0) < 3
    hi = tile.astype(BF16).astype(F32)
    low = jnp.where(keep, tile - hi, 0.0)
    tile = jnp.where(keep, hi, 0.0) + pltpu.roll(low, 3, 0)
    return jnp.concatenate([x[:ONE], tile], axis=0).astype(BF16)


def decode(x):
    x = x.astype(F32)
    tile = x[ONE:]
    keep = lax.broadcasted_iota(jnp.int32, tile.shape, 0) < 3
    tile = jnp.where(keep, tile + pltpu.roll(tile, 5, 0), 0.0)
    return jnp.concatenate([x[:ONE], tile], axis=0)


def kernel(
    n, nh, heads, total_width,
    lq_hbm, lk_hbm, lv_hbm, wq_hbm, wk_hbm, wv_hbm, cw_hbm, hg_hbm, eq_hbm, ek_hbm,
    out_ref,
    lq_ref, lk_ref, lv_ref, wq_ref, wk_ref, wv_ref, cw_ref, hg_ref, eq_ref, ek_ref,
    own, zin, xin, fwd, hk, hv, mix, num, den, phq, sq_out, sq_in,
    in_sem, z_send, z_recv, x_send, x_recv, h_send, h_recv, s_send, s_recv,
):
    count = lv_ref.shape[0]
    ctx = lax.axis_index("ctx")
    hd = lax.axis_index("head")
    z = ctx // 2
    x = lax.rem(ctx, 2)
    nz = n // 2
    partner = ctx + 1 - 2 * x

    loads = {}
    for i, (name, src, dst) in enumerate([
        ("lk", lk_hbm, lk_ref), ("ek", ek_hbm, ek_ref), ("lv", lv_hbm, lv_ref),
        ("wk", wk_hbm, wk_ref), ("wv", wv_hbm, wv_ref), ("lq", lq_hbm, lq_ref),
        ("wq", wq_hbm, wq_ref), ("eq", eq_hbm, eq_ref), ("cw", cw_hbm, cw_ref), ("hg", hg_hbm, hg_ref),
    ]):
        loads[name] = pltpu.make_async_copy(src, dst, in_sem.at[i])
        loads[name].start()

    barrier = pltpu.get_barrier_semaphore()
    peers = jnp.minimum(ctx, 2) + jnp.minimum(n - 1 - ctx, 2) + (nh - 1)

    def greet(c, h):
        pl.semaphore_signal(barrier, inc=1, device_id=(c, h), device_id_type=MESH)

    for by in (-2, -1, 1, 2):
        @pl.when((ctx + by >= 0) & (ctx + by < n))
        def _(by=by):
            greet(ctx + by, hd)
    for j in range(1, nh):
        greet(ctx, lax.rem(hd + j, nh))

    def halo(src, dst, i):
        return pltpu.make_async_remote_copy(
            src_ref=src.at[pl.ds(count - WIN, WIN)], dst_ref=dst,
            send_sem=h_send.at[i], recv_sem=h_recv.at[i],
            device_id=(ctx + 1, hd), device_id_type=MESH)

    def z_copy(h):
        return pltpu.make_async_remote_copy(
            src_ref=fwd.at[h], dst_ref=zin.at[h], send_sem=z_send.at[h], recv_sem=z_recv.at[h],
            device_id=(ctx + 2, hd), device_id_type=MESH)

    def x_copy(h, src):
        return pltpu.make_async_remote_copy(
            src_ref=src.at[h], dst_ref=xin.at[h], send_sem=x_send.at[h], recv_sem=x_recv.at[h],
            device_id=(partner, hd), device_id_type=MESH)

    def send_halos():
        @pl.when(ctx < n - 1)
        def _():
            halo(wk_ref, hk, 0).start()
            halo(wv_ref, hv, 1).start()

    def send(h):
        @pl.when(z < nz - 1)
        def _():
            z_copy(h).start()

        @pl.when(x == 0)
        def _():
            x_copy(h, fwd).start()

    def chain(h):
        z_copy(h).wait_recv()

        @pl.when(x == 1)
        def _():
            x_copy(h, zin).start()

        fwd[h] = encode(decode(zin[h]) + own[h])
        send(h)

    row_head = lax.broadcasted_iota(jnp.int32, (heads * FDIM, count), 0) // FDIM
    zero = jnp.zeros((), BF16)
    row8 = lax.broadcasted_iota(jnp.int32, (8, VDIM), 0)
    ones = jnp.ones((8, count), BF16)
    const = jnp.where(lax.broadcasted_iota(jnp.int32, (8, count), 0) == 0, 1.0, 0.0)
    loads["lk"].wait()
    loads["ek"].wait()
    lk = lk_ref[...]
    phis = []
    for h in range(heads):
        kh = jnp.where(row_head == h, lk, zero)
        ab = jnp.dot(ek_ref[...], kh, preferred_element_type=F32)
        phis.append(jnp.concatenate(
            [ab[:NP] * ab[ROWS:ROWS + NP], ab[NP:ONE], const], axis=0).astype(BF16))
    loads["lv"].wait()
    for h in range(heads):
        phi = phis[h]
        st = jnp.dot(phi, lv_ref[:, h * VDIM:(h + 1) * VDIM], preferred_element_type=F32)
        n_a = lax.dot_general(ones, phi[:VDIM], NT, preferred_element_type=F32)
        rest = jnp.concatenate([phi[VDIM:], jnp.zeros((2 * VDIM - ROWS, count), BF16)], axis=0)
        n_b = lax.dot_general(ones, rest, NT, preferred_element_type=F32)
        tile = st[ONE:] + jnp.where(row8 == 1, n_a, 0.0) + jnp.where(row8 == 2, n_b, 0.0)
        own[h] = jnp.concatenate([st[:ONE], tile], axis=0)
        if h == 0:
            loads["wk"].wait()
            loads["wv"].wait()
            pl.semaphore_wait(barrier, peers)
            pl.when(z > 0)(send_halos)

        @pl.when(z == 0)
        def _(h=h):
            fwd[h] = encode(own[h])
            send(h)

    pl.when(z == 0)(send_halos)

    @pl.when(ctx == 0)
    def _():
        hk[...] = jnp.zeros_like(hk)
        hv[...] = jnp.zeros_like(hv)

    for name in ("lq", "wq", "eq", "cw", "hg"):
        loads[name].wait()
    lq = lq_ref[...].astype(F32).T.astype(BF16)
    causal = (lax.broadcasted_iota(jnp.int32, (BLK, BLK), 0)
              >= lax.broadcasted_iota(jnp.int32, (BLK, BLK), 1))
    wr = lax.broadcasted_iota(jnp.int32, (BLK, BLK + WIN), 0)
    wc = lax.broadcasted_iota(jnp.int32, (BLK, BLK + WIN), 1)
    band = (wc > wr) & (wc <= wr + WIN)
    lane = lax.broadcasted_iota(jnp.int32, (1, 256), 1)
    add1 = jnp.where(lane == ONE, 1.0, 0.0)
    add2 = jnp.where(lane == ONE, 1.0, jnp.where((lane >= NP) & (lane < ONE), 0.25, 0.0))
    eq_head = lax.broadcasted_iota(jnp.int32, (heads * FDIM, 512), 0) // FDIM

    fan = heads * FDIM
    eq = jnp.concatenate([eq_ref[k * fan:(k + 1) * fan] for k in range(4)], axis=1)

    def inner(h):
        cols = slice(h * VDIM, (h + 1) * VDIM)
        kh = jnp.where(row_head == h, lk, zero) * jnp.asarray(0.25, BF16)
        for b in range(count // BLK):
            rows = slice(b * BLK, (b + 1) * BLK)
            s = jnp.dot(lq[rows], kh[:, :(b + 1) * BLK], preferred_element_type=F32)
            a = 1.0 + s + 0.5 * s * s
            last = jnp.where(causal, a[:, b * BLK:], 0.0)
            a = last if b == 0 else jnp.concatenate([a[:, :b * BLK], last], axis=1)
            den[h, rows] = jnp.sum(a, axis=-1, keepdims=True)
            num[rows, cols] = jnp.dot(
                a.astype(BF16), lv_ref[:(b + 1) * BLK, cols], preferred_element_type=F32)

    def query_features(h):
        e = jnp.where(eq_head == h, eq, zero)
        ab = jnp.dot(lq, e, preferred_element_type=F32)
        phq[h] = ((ab[:, :256] + add1) * (ab[:, 256:] + add2)).astype(BF16)

    def window(h, b, ext_k, ext_v, allowed):
        cols = slice(h * VDIM, (h + 1) * VDIM)
        rows = slice(b * BLK, (b + 1) * BLK)
        s = lax.dot_general(wq_ref[rows, cols], ext_k, NT, preferred_element_type=F32) * (1.0 / np.sqrt(VDIM))
        top = jnp.max(jnp.where(allowed, s, -1e30), axis=-1, keepdims=True)
        p = jnp.where(allowed, jnp.exp(s - top), 0.0)
        tot = jnp.sum(p, axis=-1, keepdims=True)
        o = jnp.dot(p.astype(BF16), ext_v, preferred_element_type=F32)
        mix[rows, cols] = o * (1.0 / tot)

    def later_blocks(h):
        cols = slice(h * VDIM, (h + 1) * VDIM)
        for b in range(1, count // BLK):
            rows = slice(b * BLK - WIN, (b + 1) * BLK)
            window(h, b, wk_ref[rows, cols], wv_ref[rows, cols], band)

    def first_block_and_conv(h):
        if h == 0:
            @pl.when(ctx > 0)
            def _():
                halo(wk_ref, hk, 0).wait_recv()
                halo(wv_ref, hv, 1).wait_recv()

        cols = slice(h * VDIM, (h + 1) * VDIM)
        ext_k = jnp.concatenate([hk[:, cols], wk_ref[:BLK, cols]], axis=0)
        ext_v = jnp.concatenate([hv[:, cols], wv_ref[:BLK, cols]], axis=0)
        window(h, 0, ext_k, ext_v, band & ((wc >= WIN) | (ctx > 0)))
        ext = jnp.concatenate([hv[WIN - 16:, cols], wv_ref[:, cols]], axis=0).astype(F32)
        taps = cw_ref[:, cols].astype(F32)
        acc = taps[0:1] * ext[16:16 + count]
        for t in range(1, TAPS):
            acc = acc + taps[t:t + 1] * ext[16 - t:16 - t + count]
        mix[:, cols] = hg_ref[:, cols] * (mix[:, cols] + acc)

    units = [functools.partial(f, h)
             for f in (inner, query_features, later_blocks, first_block_and_conv)
             for h in range(heads)]
    slots = {}
    for level, begin in ((1, 2), (2, 6), (3, 10)):
        for h in range(heads):
            slots.setdefault(min(begin + 2 * h, len(units)), []).append((level, h))
    for u in range(len(units) + 1):
        for level, h in slots.get(u, []):
            here = z == level if level < 3 else z >= level
            pl.when(here)(functools.partial(chain, h))
        if u < len(units):
            units[u]()

    squares = jnp.zeros((count, VDIM), F32)
    for h in range(heads):
        cols = slice(h * VDIM, (h + 1) * VDIM)

        @pl.when(ctx > 0)
        def _():
            x_copy(h, zin).wait_recv()

            @pl.when(z > 0)
            def _():
                own[h] = decode(zin[h]) + decode(xin[h])

            @pl.when(z == 0)
            def _():
                own[h] = decode(xin[h])

        @pl.when(ctx == 0)
        def _():
            own[h] = jnp.zeros((ROWS, VDIM), F32)

        st = own[h]
        tile = st[ONE:]
        norm = jnp.concatenate([tile[1:2], tile[2:3]], axis=1)
        state = jnp.concatenate([st[:ONE], jnp.zeros((8, VDIM), F32)], axis=0).astype(BF16)
        cross = jnp.dot(phq[h][:, :ROWS], state, preferred_element_type=F32)
        d = den[h] + jnp.sum(phq[h].astype(F32) * norm, axis=-1, keepdims=True)
        lin = (num[:, cols] + cross + tile[0:1]) * (1.0 / d)
        m = hg_ref[:, cols] * lin + mix[:, cols]
        mix[:, cols] = m
        squares = squares + m * m

    row = jnp.sum(squares.T, axis=0, keepdims=True)
    sq_out[...] = jnp.broadcast_to(row, sq_out.shape)

    def sq_copy(j):
        return pltpu.make_async_remote_copy(
            src_ref=sq_out, dst_ref=sq_in.at[j - 1], send_sem=s_send.at[j - 1], recv_sem=s_recv.at[j - 1],
            device_id=(ctx, lax.rem(hd + j, nh)), device_id_type=MESH)

    for j in range(1, nh):
        sq_copy(j).start()
    tot = sq_out[...]
    for j in range(1, nh):
        sq_copy(j).wait_recv()
        tot = tot + sq_in[j - 1]
    scale = lax.rsqrt(tot * (1.0 / total_width) + 1e-6)
    scale = jnp.broadcast_to(scale[0:1], (VDIM, count)).T
    for h in range(heads):
        cols = slice(h * VDIM, (h + 1) * VDIM)
        out_ref[:, cols] = (mix[:, cols] * scale).astype(BF16)

    for j in range(1, nh):
        sq_copy(j).wait_send()

    @pl.when(ctx < n - 1)
    def _():
        halo(wk_ref, hk, 0).wait_send()
        halo(wv_ref, hv, 1).wait_send()

    for h in range(heads):
        @pl.when(z < nz - 1)
        def _(h=h):
            z_copy(h).wait_send()

        @pl.when((x == 0) | (z > 0))
        def _(h=h):
            x_copy(h, zin).wait_send()


def body(n, nh, lq, lk, lv, wq, wk, wv, cw, hg):
    count, width = wv.shape
    heads = width // VDIM
    vmem = pl.BlockSpec(memory_space=pltpu.VMEM)
    dma = pltpu.SemaphoreType.DMA
    call = pl.pallas_call(
        functools.partial(kernel, n, nh, heads, width * nh),
        out_shape=jax.ShapeDtypeStruct((count, width), BF16),
        in_specs=[pl.BlockSpec(memory_space=pltpu.HBM)] * 10,
        out_specs=vmem,
        scratch_shapes=[
            pltpu.VMEM(lq.shape[::-1], BF16),
            pltpu.VMEM(lk.shape[::-1], BF16),
            pltpu.VMEM((count, width), BF16),
            pltpu.VMEM((count, width), BF16),
            pltpu.VMEM((count, width), BF16),
            pltpu.VMEM((count, width), BF16),
            pltpu.VMEM(cw.shape, BF16),
            pltpu.VMEM((1, width), F32),
            pltpu.VMEM((4 * heads * FDIM, VDIM), BF16),
            pltpu.VMEM((EK, heads * FDIM), BF16),
            pltpu.VMEM((heads, ROWS, VDIM), F32),
            pltpu.VMEM((heads, ROWS, VDIM), BF16),
            pltpu.VMEM((heads, ROWS, VDIM), BF16),
            pltpu.VMEM((heads, ROWS, VDIM), BF16),
            pltpu.VMEM((WIN, width), BF16),
            pltpu.VMEM((WIN, width), BF16),
            pltpu.VMEM((count, width), F32),
            pltpu.VMEM((count, width), F32),
            pltpu.VMEM((heads, count, 1), F32),
            pltpu.VMEM((heads, count, 256), BF16),
            pltpu.VMEM((8, count), F32),
            pltpu.VMEM((nh - 1, 8, count), F32),
            dma((10,)), dma((heads,)), dma((heads,)), dma((heads,)), dma((heads,)),
            dma((2,)), dma((2,)), dma((nh - 1,)), dma((nh - 1,)),
        ],
        compiler_params=pltpu.CompilerParams(
            collective_id=0, has_side_effects=True, vmem_limit_bytes=60 * 1024 * 1024
        ),
        cost_estimate=pl.CostEstimate(flops=500_000_000, bytes_accessed=3_000_000, transcendentals=200_000),
    )
    return call(lq.T, lk.T, lv, wq, wk, wv, cw, hg.reshape(1, width), *selectors(heads))


def solution(mesh):
    both = P("ctx", "head")
    placed = (both, both, both, both, both, both, P(None, "head"), P("head"))
    return jax.shard_map(
        functools.partial(body, mesh.shape["ctx"], mesh.shape["head"]),
        mesh=mesh, in_specs=placed, out_specs=both, check_vma=False,
    )
```

time: 27.9 us -> 22.2 us (0.80)
  local copies, waits for them, and re-layouts: 6.16 us -> 1.67 us
  Pallas kernels: 21.3 us -> 20.4 us
    unnamed x25 -> x1, local copies, waits for them, and re-layouts: 6.16 us -> 1.67 us
    pallas_call x1, Pallas kernels: 21.3 us -> 20.4 us  [body(): call(lq.T, lk.T, lv, wq, wk, wv, cw, hg.reshape(1, width), *selectors(hea...]
where the time goes in v2:
time: 22.2 us; the launch traced here: 22.1 us
  Pallas kernels  20.4 us (92%)
  local copies, waits for them, and re-layouts  1.67 us (8%)
    pallas_call x1, Pallas kernels, body(): call(lq.T, lk.T, lv, wq, wk, wv, cw, hg.reshape(1, width), *selectors(hea...  20.4 us
    unnamed x1, local copies, waits for them, and re-layouts  1.67 us

profile of v2, /device:TPU:25, one launch (start us, length us, event | category | flops | bytes accessed | tf_op | source)
XLA Modules:
  0.0 22.1 jit_solution(3060942189327343520)
XLA Ops:
  0.0 20.4 %shard_map.100 = bf16[256,512]{1,0:T(8,128)(2,1)} custom-call(bf16[64,256]{1,0:T(8,128)(2,1)} %bitcast.3, bf16[64,256]{1,0:T(8,128)(2,1)} %bitcast.4, bf16[256,512]{1,0:T(8,128)(2,1)} %lv_hbm.1, bf16[256,512]{1,0:T(8,128)(2,1)} %wq_hbm.1, bf16[256,512]{1,0:T(8,128)(2,1)} %wk_hbm.1, bf16[256,512]{1,0:T(8,128)(2,1)} %wv_hbm.1, bf16[3,512]{1,0:T(4,128)(2,1)} %cw_hbm.1, ...), custom_call_target="tpu_custom_call" | custom-call | flops 500000000 | bytes 3000000 | tf_op jit(solution)/shard_map/pallas_call | solution.py:376
  20.4 1.7 %copy.12 = bf16[256,512]{1,0:T(8,128)(2,1)} copy(bf16[256,512]{1,0:T(8,128)(2,1)} %shard_map.100) | data formatting | bytes 524288

commit v3 on v2

--- a/solution.py
+++ b/solution.py
@@ -121,11 +121,12 @@
             halo(wk_ref, hk, 0).start()
             halo(wv_ref, hv, 1).start()
 
-    def send(h):
+    def send_z(h):
         @pl.when(z < nz - 1)
         def _():
             z_copy(h).start()
 
+    def send_x(h):
         @pl.when(x == 0)
         def _():
             x_copy(h, fwd).start()
@@ -138,7 +139,8 @@
             x_copy(h, zin).start()
 
         fwd[h] = encode(decode(zin[h]) + own[h])
-        send(h)
+        send_z(h)
+        send_x(h)
 
     row_head = lax.broadcasted_iota(jnp.int32, (heads * FDIM, count), 0) // FDIM
     zero = jnp.zeros((), BF16)
@@ -162,24 +164,42 @@
         rest = jnp.concatenate([phi[VDIM:], jnp.zeros((2 * VDIM - ROWS, count), BF16)], axis=0)
         n_b = lax.dot_general(ones, rest, NT, preferred_element_type=F32)
         tile = st[ONE:] + jnp.where(row8 == 1, n_a, 0.0) + jnp.where(row8 == 2, n_b, 0.0)
-        own[h] = jnp.concatenate([st[:ONE], tile], axis=0)
-        if h == 0:
+        st = jnp.concatenate([st[:ONE], tile], axis=0)
+        own[h] = st
+        fwd[h] = encode(st)
+        if h == min(1, heads - 1):
             loads["wk"].wait()
             loads["wv"].wait()
             pl.semaphore_wait(barrier, peers)
-            pl.when(z > 0)(send_halos)
-
-        @pl.when(z == 0)
-        def _(h=h):
-            fwd[h] = encode(own[h])
-            send(h)
-
-    pl.when(z == 0)(send_halos)
+
+            @pl.when(z == 0)
+            def _():
+                for g in range(h):
+                    send_z(g)
+
+            pl.when((z > 0) | (x == 0))(send_halos)
+
+            @pl.when(z == 0)
+            def _():
+                for g in range(h):
+                    send_x(g)
+        if h >= min(1, heads - 1):
+            @pl.when(z == 0)
+            def _(h=h):
+                send_z(h)
+                send_x(h)
+
+    pl.when(ctx == 1)(send_halos)
+
+    @pl.when(z == 0)
+    def _():
+        zin[...] = jnp.zeros_like(zin)
 
     @pl.when(ctx == 0)
     def _():
         hk[...] = jnp.zeros_like(hk)
         hv[...] = jnp.zeros_like(hv)
+        xin[...] = jnp.zeros_like(xin)
 
     for name in ("lq", "wq", "eq", "cw", "hg"):
         loads[name].wait()
@@ -232,12 +252,6 @@
             window(h, b, wk_ref[rows, cols], wv_ref[rows, cols], band)
 
     def first_block_and_conv(h):
-        if h == 0:
-            @pl.when(ctx > 0)
-            def _():
-                halo(wk_ref, hk, 0).wait_recv()
-                halo(wv_ref, hv, 1).wait_recv()
-
         cols = slice(h * VDIM, (h + 1) * VDIM)
         ext_k = jnp.concatenate([hk[:, cols], wk_ref[:BLK, cols]], axis=0)
         ext_v = jnp.concatenate([hv[:, cols], wv_ref[:BLK, cols]], axis=0)
@@ -249,19 +263,25 @@
             acc = acc + taps[t:t + 1] * ext[16 - t:16 - t + count]
         mix[:, cols] = hg_ref[:, cols] * (mix[:, cols] + acc)
 
-    units = [functools.partial(f, h)
-             for f in (inner, query_features, later_blocks, first_block_and_conv)
-             for h in range(heads)]
-    slots = {}
-    for level, begin in ((1, 2), (2, 6), (3, 10)):
+    def chain_all():
         for h in range(heads):
-            slots.setdefault(min(begin + 2 * h, len(units)), []).append((level, h))
-    for u in range(len(units) + 1):
-        for level, h in slots.get(u, []):
-            here = z == level if level < 3 else z >= level
-            pl.when(here)(functools.partial(chain, h))
-        if u < len(units):
-            units[u]()
+            chain(h)
+
+    pl.when(z == 1)(chain_all)
+    for h in range(heads):
+        inner(h)
+        query_features(h)
+        later_blocks(h)
+    pl.when(z == 2)(chain_all)
+
+    @pl.when(ctx > 0)
+    def _():
+        halo(wk_ref, hk, 0).wait_recv()
+        halo(wv_ref, hv, 1).wait_recv()
+
+    for h in range(heads):
+        first_block_and_conv(h)
+    pl.when(z > 2)(chain_all)
 
     squares = jnp.zeros((count, VDIM), F32)
     for h in range(heads):
@@ -271,19 +291,7 @@
         def _():
             x_copy(h, zin).wait_recv()
 
-            @pl.when(z > 0)
-            def _():
-                own[h] = decode(zin[h]) + decode(xin[h])
-
-            @pl.when(z == 0)
-            def _():
-                own[h] = decode(xin[h])
-
-        @pl.when(ctx == 0)
-        def _():
-            own[h] = jnp.zeros((ROWS, VDIM), F32)
-
-        st = own[h]
+        st = decode(zin[h]) + decode(xin[h])
         tile = st[ONE:]
         norm = jnp.concatenate([tile[1:2], tile[2:3]], axis=1)
         state = jnp.concatenate([st[:ONE], jnp.zeros((8, VDIM), F32)], axis=0).astype(BF16)
@@ -369,7 +377,7 @@
             dma((2,)), dma((2,)), dma((nh - 1,)), dma((nh - 1,)),
         ],
         compiler_params=pltpu.CompilerParams(
-            collective_id=0, has_side_effects=True, vmem_limit_bytes=60 * 1024 * 1024
+            collective_id=0, has_side_effects=True, vmem_limit_bytes=54528 * 1024
         ),
         cost_estimate=pl.CostEstimate(flops=500_000_000, bytes_accessed=3_000_000, transcendentals=200_000),
     )

time: 22.2 us -> 25.6 us (1.15)
  local copies, waits for them, and re-layouts: 1.67 us -> 5.31 us
  Pallas kernels: 20.4 us -> 19.9 us
    unnamed x1 -> x13, local copies, waits for them, and re-layouts: 1.67 us -> 5.31 us
    pallas_call x1, Pallas kernels: 20.4 us -> 19.9 us  [body(): call(lq.T, lk.T, lv, wq, wk, wv, cw, hg.reshape(1, width), *selectors(hea...]
where the time goes in v3:
time: 25.6 us; the launch traced here: 25.2 us
  Pallas kernels  19.9 us (78%)
  local copies, waits for them, and re-layouts  5.31 us (21%)
    pallas_call x1, Pallas kernels, body(): call(lq.T, lk.T, lv, wq, wk, wv, cw, hg.reshape(1, width), *selectors(hea...  19.9 us
    unnamed x13, local copies, waits for them, and re-layouts  5.31 us

profile of v3, /device:TPU:25, one launch (start us, length us, event | category | flops | bytes accessed | tf_op | source)
XLA Modules:
  0.0 25.2 jit_solution(8184415548379404992)
XLA Ops:
  0.0 0.0 copy-start.2
  0.0 0.7 %copy-done.2 = bf16[3,512]{1,0:T(4,128)(2,1)S(1)} copy-done((bf16[3,512]{1,0:T(4,128)(2,1)S(1)}, bf16[3,512]{1,0:T(4,128)(2,1)}, u32[]{:S(2)}) %copy-start.2) | copy-done | bytes 3096
  0.7 0.0 copy-start
  0.7 0.8 %copy-done = bf16[256,64]{0,1:T(8,128)(2,1)S(1)} copy-done((bf16[256,64]{0,1:T(8,128)(2,1)S(1)}, bf16[256,64]{0,1:T(8,128)(2,1)}, u32[]{:S(2)}) %copy-start) | copy-done | bytes 32792
  1.4 0.0 copy-start.1
  1.4 0.8 %copy-done.1 = bf16[256,64]{0,1:T(8,128)(2,1)S(1)} copy-done((bf16[256,64]{0,1:T(8,128)(2,1)S(1)}, bf16[256,64]{0,1:T(8,128)(2,1)}, u32[]{:S(2)}) %copy-start.1) | copy-done | bytes 32792
  2.2 0.0 copy-start.3
  2.2 0.7 %copy-done.3 = f32[512]{0:T(512)S(1)} copy-done((f32[512]{0:T(512)S(1)}, f32[512]{0:T(512)}, u32[]{:S(2)}) %copy-start.3) | copy-done | bytes 2072
  2.9 0.0 copy-start.4
  2.9 0.9 %copy-done.4 = bf16[304,64]{1,0:T(8,128)(2,1)S(1)} copy-done((bf16[304,64]{1,0:T(8,128)(2,1)S(1)}, bf16[304,64]{1,0:T(8,128)(2,1)}, u32[]{:S(2)}) %copy-start.4) | copy-done | bytes 38936
  3.8 0.0 copy-start.5
  3.8 0.8 %copy-done.5 = bf16[256,128]{1,0:T(8,128)(2,1)S(1)} copy-done((bf16[256,128]{1,0:T(8,128)(2,1)S(1)}, bf16[256,128]{1,0:T(8,128)(2,1)}, u32[]{:S(2)}) %copy-start.5) | copy-done | bytes 65560
  4.6 19.9 %shard_map.100 = bf16[256,512]{1,0:T(8,128)(2,1)S(1)} custom-call(bf16[64,256]{1,0:T(8,128)(2,1)S(1)} %bitcast.3, bf16[64,256]{1,0:T(8,128)(2,1)S(1)} %bitcast.4, bf16[256,512]{1,0:T(8,128)(2,1)} %lv_hbm.1, bf16[256,512]{1,0:T(8,128)(2,1)} %wq_hbm.1, bf16[256,512]{1,0:T(8,128)(2,1)} %wk_hbm.1, bf16[256,512]{1,0:T(8,128)(2,1)} %wv_hbm.1, ...), custom_call_target="tpu_custom_call" | custom-call | flops 500000000 | bytes 3000000 | tf_op jit(solution)/shard_map/pallas_call | solution.py:384
  24.5 0.7 %copy.12 = bf16[256,512]{1,0:T(8,128)(2,1)} copy(bf16[256,512]{1,0:T(8,128)(2,1)S(1)} %shard_map.100) | data formatting | bytes 524288
Async XLA Ops:
  0.0 0.7 %copy-start.2 = (bf16[3,512]{1,0:T(4,128)(2,1)S(1)}, bf16[3,512]{1,0:T(4,128)(2,1)}, u32[]{:S(2)}) copy-start(bf16[3,512]{1,0:T(4,128)(2,1)} %cw_hbm.1) | copy-start | bytes 9220
  0.7 0.8 %copy-start = (bf16[256,64]{0,1:T(8,128)(2,1)S(1)}, bf16[256,64]{0,1:T(8,128)(2,1)}, u32[]{:S(2)}) copy-start(bf16[256,64]{0,1:T(8,128)(2,1)} %param.10) | copy-start | bytes 98308
  1.4 0.8 %copy-start.1 = (bf16[256,64]{0,1:T(8,128)(2,1)S(1)}, bf16[256,64]{0,1:T(8,128)(2,1)}, u32[]{:S(2)}) copy-start(bf16[256,64]{0,1:T(8,128)(2,1)} %param.11) | copy-start | bytes 98308
  2.2 0.7 %copy-start.3 = (f32[512]{0:T(512)S(1)}, f32[512]{0:T(512)}, u32[]{:S(2)}) copy-start(f32[512]{0:T(512)} %param.17) | copy-start | bytes 6148
  2.9 0.9 %copy-start.4 = (bf16[304,64]{1,0:T(8,128)(2,1)S(1)}, bf16[304,64]{1,0:T(8,128)(2,1)}, u32[]{:S(2)}) copy-start(bf16[304,64]{1,0:T(8,128)(2,1)} %constant.5.clone.ek_hbm) | copy-start | bytes 116740
  3.8 0.8 %copy-start.5 = (bf16[256,128]{1,0:T(8,128)(2,1)S(1)}, bf16[256,128]{1,0:T(8,128)(2,1)}, u32[]{:S(2)}) copy-start(bf16[256,128]{1,0:T(8,128)(2,1)} %constant.4.clone.eq_hbm) | copy-start | bytes 196612

commit v4 on v3

--- a/solution.py
+++ b/solution.py
@@ -18,6 +18,7 @@
 ONE = NP + FDIM
 ROWS = ONE + 8
 EK = ROWS + 144
+HALF = ROWS // 2
 MESH = pl.DeviceIdType.MESH
 F32 = jnp.float32
 BF16 = jnp.bfloat16
@@ -45,20 +46,20 @@
 
 
 def encode(x):
-    tile = x[ONE:]
+    tile = x[-8:]
     keep = lax.broadcasted_iota(jnp.int32, tile.shape, 0) < 3
     hi = tile.astype(BF16).astype(F32)
     low = jnp.where(keep, tile - hi, 0.0)
     tile = jnp.where(keep, hi, 0.0) + pltpu.roll(low, 3, 0)
-    return jnp.concatenate([x[:ONE], tile], axis=0).astype(BF16)
+    return jnp.concatenate([x[:-8], tile], axis=0).astype(BF16)
 
 
 def decode(x):
     x = x.astype(F32)
-    tile = x[ONE:]
+    tile = x[-8:]
     keep = lax.broadcasted_iota(jnp.int32, tile.shape, 0) < 3
     tile = jnp.where(keep, tile + pltpu.roll(tile, 5, 0), 0.0)
-    return jnp.concatenate([x[:ONE], tile], axis=0)
+    return jnp.concatenate([x[:-8], tile], axis=0)
 
 
 def kernel(
@@ -105,14 +106,17 @@
             send_sem=h_send.at[i], recv_sem=h_recv.at[i],
             device_id=(ctx + 1, hd), device_id_type=MESH)
 
-    def z_copy(h):
+    def part(ref, c):
+        return ref.at[c // 2, pl.ds(c % 2 * HALF, HALF)]
+
+    def z_copy(c):
         return pltpu.make_async_remote_copy(
-            src_ref=fwd.at[h], dst_ref=zin.at[h], send_sem=z_send.at[h], recv_sem=z_recv.at[h],
+            src_ref=part(fwd, c), dst_ref=part(zin, c), send_sem=z_send.at[c], recv_sem=z_recv.at[c],
             device_id=(ctx + 2, hd), device_id_type=MESH)
 
-    def x_copy(h, src):
+    def x_copy(c, src):
         return pltpu.make_async_remote_copy(
-            src_ref=src.at[h], dst_ref=xin.at[h], send_sem=x_send.at[h], recv_sem=x_recv.at[h],
+            src_ref=part(src, c), dst_ref=part(xin, c), send_sem=x_send.at[c], recv_sem=x_recv.at[c],
             device_id=(partner, hd), device_id_type=MESH)
 
     def send_halos():
@@ -124,23 +128,35 @@
     def send_z(h):
         @pl.when(z < nz - 1)
         def _():
-            z_copy(h).start()
+            z_copy(2 * h).start()
+            z_copy(2 * h + 1).start()
 
     def send_x(h):
         @pl.when(x == 0)
         def _():
-            x_copy(h, fwd).start()
-
-    def chain(h):
-        z_copy(h).wait_recv()
+            x_copy(2 * h, fwd).start()
+            x_copy(2 * h + 1, fwd).start()
+
+    def chain(c):
+        h, rows = c // 2, slice(c % 2 * HALF, (c % 2 + 1) * HALF)
+        z_copy(c).wait_recv()
 
         @pl.when(x == 1)
         def _():
-            x_copy(h, zin).start()
-
-        fwd[h] = encode(decode(zin[h]) + own[h])
-        send_z(h)
-        send_x(h)
+            x_copy(c, zin).start()
+
+        if c % 2:
+            fwd[h, rows] = encode(decode(zin[h, rows]) + own[h, rows])
+        else:
+            fwd[h, rows] = (zin[h, rows].astype(F32) + own[h, rows]).astype(BF16)
+
+        @pl.when(z < nz - 1)
+        def _():
+            z_copy(c).start()
+
+        @pl.when(x == 0)
+        def _():
+            x_copy(c, fwd).start()
 
     row_head = lax.broadcasted_iota(jnp.int32, (heads * FDIM, count), 0) // FDIM
     zero = jnp.zeros((), BF16)
@@ -264,8 +280,8 @@
         mix[:, cols] = hg_ref[:, cols] * (mix[:, cols] + acc)
 
     def chain_all():
-        for h in range(heads):
-            chain(h)
+        for c in range(2 * heads):
+            chain(c)
 
     pl.when(z == 1)(chain_all)
     for h in range(heads):
@@ -289,7 +305,8 @@
 
         @pl.when(ctx > 0)
         def _():
-            x_copy(h, zin).wait_recv()
+            x_copy(2 * h, zin).wait_recv()
+            x_copy(2 * h + 1, zin).wait_recv()
 
         st = decode(zin[h]) + decode(xin[h])
         tile = st[ONE:]
@@ -330,14 +347,14 @@
         halo(wk_ref, hk, 0).wait_send()
         halo(wv_ref, hv, 1).wait_send()
 
-    for h in range(heads):
+    for c in range(2 * heads):
         @pl.when(z < nz - 1)
-        def _(h=h):
-            z_copy(h).wait_send()
+        def _(c=c):
+            z_copy(c).wait_send()
 
         @pl.when((x == 0) | (z > 0))
-        def _(h=h):
-            x_copy(h, zin).wait_send()
+        def _(c=c):
+            x_copy(c, zin).wait_send()
 
 
 def body(n, nh, lq, lk, lv, wq, wk, wv, cw, hg):
@@ -373,11 +390,11 @@
             pltpu.VMEM((heads, count, 256), BF16),
             pltpu.VMEM((8, count), F32),
             pltpu.VMEM((nh - 1, 8, count), F32),
-            dma((10,)), dma((heads,)), dma((heads,)), dma((heads,)), dma((heads,)),
+            dma((10,)), dma((2 * heads,)), dma((2 * heads,)), dma((2 * heads,)), dma((2 * heads,)),
             dma((2,)), dma((2,)), dma((nh - 1,)), dma((nh - 1,)),
         ],
         compiler_params=pltpu.CompilerParams(
-            collective_id=0, has_side_effects=True, vmem_limit_bytes=54528 * 1024
+            collective_id=0, has_side_effects=True, vmem_limit_bytes=60 * 1024 * 1024
         ),
         cost_estimate=pl.CostEstimate(flops=500_000_000, bytes_accessed=3_000_000, transcendentals=200_000),
     )

time: 25.6 us -> 21.6 us (0.84); the launches traced: 25.2 us -> 21.5 us
  local copies, waits for them, and re-layouts: 5.31 us -> 1.67 us
    unnamed x13 -> x1, local copies, waits for them, and re-layouts: 5.31 us -> 1.67 us
where the time goes in v4:
time: 21.6 us; the launch traced here: 21.5 us
  Pallas kernels  19.8 us (92%)
  local copies, waits for them, and re-layouts  1.67 us (8%)
    pallas_call x1, Pallas kernels, body(): call(lq.T, lk.T, lv, wq, wk, wv, cw, hg.reshape(1, width), *selectors(hea...  19.8 us
    unnamed x1, local copies, waits for them, and re-layouts  1.67 us

profile of v4, /device:TPU:25, one launch (start us, length us, event | category | flops | bytes accessed | tf_op | source)
XLA Modules:
  0.0 21.5 jit_solution(16256114105979974400)
XLA Ops:
  0.0 19.8 %shard_map.100 = bf16[256,512]{1,0:T(8,128)(2,1)} custom-call(bf16[64,256]{1,0:T(8,128)(2,1)} %bitcast.3, bf16[64,256]{1,0:T(8,128)(2,1)} %bitcast.4, bf16[256,512]{1,0:T(8,128)(2,1)} %lv_hbm.1, bf16[256,512]{1,0:T(8,128)(2,1)} %wq_hbm.1, bf16[256,512]{1,0:T(8,128)(2,1)} %wk_hbm.1, bf16[256,512]{1,0:T(8,128)(2,1)} %wv_hbm.1, bf16[3,512]{1,0:T(4,128)(2,1)} %cw_hbm.1, ...), custom_call_target="tpu_custom_call" | custom-call | flops 500000000 | bytes 3000000 | tf_op jit(solution)/shard_map/pallas_call | solution.py:401
  19.8 1.7 %copy.12 = bf16[256,512]{1,0:T(8,128)(2,1)} copy(bf16[256,512]{1,0:T(8,128)(2,1)} %shard_map.100) | data formatting | bytes 524288
